TPU v7x, 128 devices: a whole 4x4x4 slice. The times are simulated.
128 devices in a mesh: row: 8 (over y, core), col: 8 (over x_hi, z), head: 2 (over x_lo).
Axes of the slice: x: 4 (x_hi: 2, x_lo: 2; x = x_hi * 2 + x_lo), y: 4, z: 4, core: 2. Of those that a mesh axis runs over, the one named last changes fastest.
Arguments:
- queries: bfloat16 [6144, 4096], P('row', ('head', 'col')), may hold values from -10 to 10
- key_states: bfloat16 [6144, 4096], P('col', ('head', 'row')), may hold values from -10 to 10
- value_states: bfloat16 [6144, 4096], P('col', ('head', 'row')), may hold values from -6 to 6
- out_grad: bfloat16 [6144, 4096], P('row', ('head', 'col')), may hold values from -6 to 6
Outputs:
- query_grad: bfloat16 [6144, 4096], P('row', ('head', 'col'))
- key_grad: bfloat16 [6144, 4096], P('col', ('head', 'row'))
- value_grad: bfloat16 [6144, 4096], P('col', ('head', 'row'))
All inputs are finite; a program needn't handle non-finite values.
Results may differ from a plain program's by a relative error of at most 0.0069.
Values may be sent and summed in bfloat16 or wider, within the bound.
A program may use at most 128 MiB of HBM per device.

v0:
```python
import math

import jax
import jax.numpy as jnp
from jax import lax
from jax.sharding import PartitionSpec as P

HEAD_DIM = 128


def per_device(queries, key_states, value_states, out_grad):
    query_all, grad_all = (
        lax.all_gather(queries, "col", axis=1, tiled=True),
        lax.all_gather(out_grad, "col", axis=1, tiled=True),
    )
    key_all, value_all = (
        lax.all_gather(key_states, "row", axis=1, tiled=True),
        lax.all_gather(value_states, "row", axis=1, tiled=True),
    )
    count = query_all.shape[1] // HEAD_DIM
    scaling = 1.0 / math.sqrt(HEAD_DIM)
    indices = jnp.arange(count, dtype=jnp.int32)
    contract_last = (((1,), (1,)), ((), ()))
    contract_first = (((0,), (0,)), ((), ()))

    def columns(array, head_index):
        return lax.dynamic_slice_in_dim(array, head_index * HEAD_DIM, HEAD_DIM, 1)

    def scores_of(head_index):
        return scaling * lax.dot_general(
            columns(query_all, head_index),
            columns(key_all, head_index),
            contract_last,
            preferred_element_type=jnp.float32,
        )

    def upstream(head_index):
        return lax.dot_general(
            columns(grad_all, head_index),
            columns(value_all, head_index),
            contract_last,
            preferred_element_type=jnp.float32,
        )

    def local_peak(head_index):
        scores = scores_of(head_index)
        peak = jnp.max(scores, axis=1)
        return (peak, jnp.sum(jnp.exp(scores - peak[:, None]), axis=1))

    peak_loc, total_loc = lax.map(local_peak, indices)
    peak = lax.pmax(peak_loc.astype(jnp.bfloat16), "col").astype(peak_loc.dtype)
    total = lax.psum(total_loc * jnp.exp(peak_loc - peak), "col")

    def local_delta(head_index):
        prob = (
            jnp.exp(scores_of(head_index) - peak[head_index][:, None]) / total[head_index][:, None]
        )
        return jnp.sum(prob * upstream(head_index), axis=1)

    delta = lax.psum(lax.map(local_delta, indices), "col")

    def tile_terms(head_index):
        prob = (
            jnp.exp(scores_of(head_index) - peak[head_index][:, None]) / total[head_index][:, None]
        )
        dprob = upstream(head_index)
        dscore = (prob * (dprob - delta[head_index][:, None]) * scaling).astype(jnp.bfloat16)
        return (prob.astype(jnp.bfloat16), dscore)

    query_zero = jnp.zeros(query_all.shape, jnp.float32)
    key_zero = jnp.zeros(key_all.shape, jnp.float32)

    def accumulate(head_index, carry):
        query_acc, key_acc, value_acc = carry
        prob_low, dscore = tile_terms(head_index)
        value_term = lax.dot_general(
            prob_low,
            columns(grad_all, head_index),
            contract_first,
            preferred_element_type=jnp.float32,
        )
        query_term = jnp.dot(
            dscore, columns(key_all, head_index), preferred_element_type=jnp.float32
        )
        key_term = lax.dot_general(
            dscore,
            columns(query_all, head_index),
            contract_first,
            preferred_element_type=jnp.float32,
        )
        start = head_index * HEAD_DIM
        query_acc = lax.dynamic_update_slice_in_dim(query_acc, query_term, start, 1)
        key_acc = lax.dynamic_update_slice_in_dim(key_acc, key_term, start, 1)
        value_acc = lax.dynamic_update_slice_in_dim(value_acc, value_term, start, 1)
        return (query_acc, key_acc, value_acc)

    query_acc, key_acc, value_acc = lax.fori_loop(
        0, count, accumulate, (query_zero, key_zero, key_zero)
    )
    key_sum, value_sum = (
        lax.psum_scatter(key_acc, "row", scatter_dimension=1, tiled=True),
        lax.psum_scatter(value_acc, "row", scatter_dimension=1, tiled=True),
    )
    query_grad = lax.psum_scatter(query_acc, "col", scatter_dimension=1, tiled=True).astype(
        jnp.bfloat16
    )
    return (query_grad, key_sum.astype(jnp.bfloat16), value_sum.astype(jnp.bfloat16))


def solution(mesh):
    placed = (
        P("row", ("head", "col")),
        P("col", ("head", "row")),
        P("col", ("head", "row")),
        P("row", ("head", "col")),
    )
    return jax.shard_map(
        per_device,
        mesh=mesh,
        in_specs=placed,
        out_specs=(P("row", ("head", "col")), P("col", ("head", "row")), P("col", ("head", "row"))),
        check_vma=False,
    )
```

profile of v0, /device:TPU:3, one launch (start us, length us, event | category | flops | bytes accessed | tf_op | source)
XLA Modules:
  0.0 749.5 jit_solution(12709857414149709408)
XLA Ops:
  10.0 65.3 %all-gather.5.cloned.1.call-done = bf16[768,2048]{1,0:T(8,128)(2,1)} async-done(((bf16[768,256]{1,0:T(8,128)(2,1)}), bf16[768,2048]{1,0:T(8,128)(2,1)}) %all-gather.5.cloned.1.call-update) | async-done | bytes 3145744 | tf_op jit(solution)/shard_map/all_gather | solution.py:13
  75.3 32.9 %all-gather.7.cloned.1.call-done = bf16[768,2048]{1,0:T(8,128)(2,1)} async-done(((bf16[768,256]{1,0:T(8,128)(2,1)}), bf16[768,2048]{1,0:T(8,128)(2,1)}) %all-gather.7.cloned.1.call-update) | async-done | bytes 3145744 | tf_op jit(solution)/shard_map/all_gather | solution.py:17
  108.3 56.6 %while.39 = (s32[]{:T(128)}, f32[16,768]{1,0:T(8,128)S(1)}, f32[16,768]{1,0:T(8,128)S(1)}, s32[16]{0:T(128)S(1)}, bf16[768,2048]{1,0:T(8,128)(2,1)}, /*index=5*/...) while((s32[]{:T(128)}, f32[16,768]{1,0:T(8,128)S(1)}, f32[16,768]{1,0:T(8,128)S(1)}, ...), condition=%wide.region_3.4_spmd, body=%wide.region_0.3_spmd.sunk | while | flops 153942528 | bytes 5146799 | solution.py:50
  164.9 34.2 %pmax.7 = bf16[16,768]{1,0:T(8,128)(2,1)S(1)} all-reduce(bf16[16,768]{1,0:T(8,128)(2,1)S(1)} %convert_element_type.29), channel_id=1, replica_groups=mesh['row'=8,'col'=8,'head'=2] {'col'}, use_global_device_ids=true, to_apply=%region_4.5 | all-reduce | flops 12288 | bytes 49152 | tf_op jit(solution)/shard_map/pmax | solution.py:51
  199.1 30.3 %psum.14 = f32[16,768]{1,0:T(8,128)S(1)} all-reduce(f32[16,768]{1,0:T(8,128)S(1)} %exponential_multiply_fusion), channel_id=1, replica_groups=mesh['row'=8,'col'=8,'head'=2] {'col'}, use_global_device_ids=true, to_apply=%region_5.6 | all-reduce | flops 12288 | bytes 98304 | tf_op jit(solution)/shard_map/psum | solution.py:52
  229.5 104.7 %while.40 = (s32[]{:T(128)}, f32[16,768]{1,0:T(8,128)S(1)}, s32[16]{0:T(128)S(1)}, bf16[768,2048]{1,0:T(8,128)(2,1)}, bf16[768,2048]{1,0:T(8,128)(2,1)}, /*index...) while((s32[]{:T(128)}, f32[16,768]{1,0:T(8,128)S(1)}, ...), condition=%wide.region_8.9_spmd, body=%wide.region_6.8_spmd.sunk | while | flops 304938240 | bytes 5541105 | solution.py:60
  334.2 31.4 %psum.15 = f32[16,768]{1,0:T(8,128)S(1)} all-reduce(f32[16,768]{1,0:T(8,128)S(1)} %get-tuple-element.271), channel_id=1, replica_groups=mesh['row'=8,'col'=8,'head'=2] {'col'}, use_global_device_ids=true, to_apply=%region_9.10 | all-reduce | flops 12288 | bytes 98304 | tf_op jit(solution)/shard_map/psum | solution.py:60
  365.6 3.4 broadcast.20.clone.1
  369.0 3.4 broadcast.20.clone
  372.4 3.4 broadcast.20
  375.8 158.9 %while.41 = (s32[]{:T(128)}, f32[768,2048]{1,0:T(8,128)}, f32[768,2048]{1,0:T(8,128)}, f32[768,2048]{1,0:T(8,128)}, bf16[768,2048]{1,0:T(8,128)(2,1)}, /*index=5...) while((s32[]{:T(128)}, f32[768,2048]{1,0:T(8,128)}, ...), condition=%wide.region_11.12_spmd, body=%wide.region_10.11_spmd.sunk | while | flops 759693312 | bytes 13205707 | solution.py:97
  381.3 2.2 convolution_dynamic-update-slice_fusion.7
  413.3 2.2 convolution_dynamic-update-slice_fusion.6
  418.8 2.2 convolution_dynamic-update-slice_fusion.8
  421.0 2.2 convolution_dynamic-update-slice_fusion.7
  448.6 2.2 convolution_dynamic-update-slice_fusion.8
  450.8 2.2 convolution_dynamic-update-slice_fusion.7
  470.6 2.2 convolution_dynamic-update-slice_fusion.7
  478.3 2.3 convolution_dynamic-update-slice_fusion.8
  488.2 2.2 convolution_dynamic-update-slice_fusion.8
  498.2 2.2 convolution_dynamic-update-slice_fusion.8
  500.4 2.2 convolution_dynamic-update-slice_fusion.7
  502.6 2.2 convolution_dynamic-update-slice_fusion.6
  508.1 2.2 convolution_dynamic-update-slice_fusion.8
  518.0 2.2 convolution_dynamic-update-slice_fusion.8
  520.3 2.2 convolution_dynamic-update-slice_fusion.7
  528.0 2.3 convolution_dynamic-update-slice_fusion.8
  530.2 2.2 convolution_dynamic-update-slice_fusion.7
  532.5 2.2 convolution_dynamic-update-slice_fusion.6
  536.1 59.5 %reduce-scatter.8.cloned.1.call-done = f32[768,256]{1,0:T(8,128)} async-done(((f32[768,2048]{1,0:T(8,128)}), f32[768,256]{1,0:T(8,128)}) %reduce-scatter.8.cloned.1.call-update) | async-done | bytes 786448 | tf_op jit(solution)/shard_map/reduce_scatter | solution.py:102
  597.5 99.1 %reduce-scatter.4.cloned.1.call-done = f32[768,256]{1,0:T(8,128)} async-done(((f32[768,2048]{1,0:T(8,128)}), f32[768,256]{1,0:T(8,128)}) %reduce-scatter.4.cloned.1.call-update) | async-done | bytes 786448 | tf_op jit(solution)/shard_map/reduce_scatter | solution.py:104
  698.5 42.2 %reduce-scatter.6.cloned.1.call-done = f32[768,256]{1,0:T(8,128)} async-done(((f32[768,2048]{1,0:T(8,128)}), f32[768,256]{1,0:T(8,128)}) %reduce-scatter.6.cloned.1.call-update) | async-done | bytes 786448 | tf_op jit(solution)/shard_map/reduce_scatter | solution.py:101
  (329 shorter events, 235.1 us)
Async XLA Ops:
  7.2 68.2 %all-gather.5.cloned.1.call-start = ((), (), s32[]{:S(2)}) async-start(), calls=%async_computation.3 | async-start | bytes 3538944 | tf_op jit(solution)/shard_map/all_gather | solution.py:13
  7.9 100.3 %all-gather.7.cloned.1.call-start = ((), (), s32[]{:S(2)}) async-start(), calls=%async_computation.4 | async-start | bytes 3538944 | tf_op jit(solution)/shard_map/all_gather | solution.py:17
  8.6 220.8 %all-gather.11.cloned.1.call-start = ((), (), s32[]{:S(2)}) async-start(), calls=%async_computation.6 | async-start | bytes 3538944 | tf_op jit(solution)/shard_map/all_gather | solution.py:18
  9.4 220.1 %all-gather.9.cloned.1.call-start = ((), (), s32[]{:S(2)}) async-start(), calls=%async_computation.5 | async-start | bytes 3538944 | tf_op jit(solution)/shard_map/all_gather | solution.py:14
  10.0 585.6 %reduce-scatter.8.cloned.1.call-start = ((), (), s32[]{:S(2)}) async-start(), calls=%async_computation.9 | async-start | bytes 7077888 | tf_op jit(solution)/shard_map/reduce_scatter | solution.py:102
  534.8 161.8 %reduce-scatter.4.cloned.1.call-start = ((), (), s32[]{:S(2)}) async-start(), calls=%async_computation.7 | async-start | bytes 7077888 | tf_op jit(solution)/shard_map/reduce_scatter | solution.py:104
  535.3 205.4 %reduce-scatter.6.cloned.1.call-start = ((), (), s32[]{:S(2)}) async-start(), calls=%async_computation.8 | async-start | bytes 7077888 | tf_op jit(solution)/shard_map/reduce_scatter | solution.py:101
Sparse Core Ops, SparseCore 0:
  10.2 65.1 all-gather.4
  77.0 31.1 all-gather.6
  109.9 32.6 all-gather.10
  144.6 63.7 all-gather.8
  534.9 60.6 reduce-scatter.7
  599.3 97.2 reduce-scatter.3
  699.0 41.6 reduce-scatter.5
where the time goes:
time: 754 us; the launch traced here: 749 us
  waiting for transfers between devices  303 us (40%)
  matrix products  233 us (31%)
  blocking collectives  95.9 us (13%)
  loops' own time  54.7 us (7%)
  local copies, waits for them, and re-layouts  36 us (5%)
  between operations  14.2 us (2%)
  other arithmetic  12.6 us (2%)
    reduce_scatter x1, waiting for transfers between devices, per_device(): lax.psum_scatter(query_acc, 'col', scatter_dimension=1, tiled=True)  99.1 us
    dot_general x48, matrix products, scores_of(): lax.dot_general(columns(query_all, head_index), columns(key_all, head_ind...  74.9 us
    all_gather x1, waiting for transfers between devices, per_device(): lax.all_gather(queries, 'col', axis=1, tiled=True)  65.3 us
    reduce_scatter x1, waiting for transfers between devices, per_device(): lax.psum_scatter(value_acc, 'row', scatter_dimension=1, tiled=True)  59.5 us
    dot_general x32, matrix products, upstream(): lax.dot_general(columns(grad_all, head_index), columns(value_all, head_in...  51.5 us
    another operation x1, loops' own time, per_device(): delta = lax.psum(lax.map(local_delta, indices), 'col')  42.3 us
    reduce_scatter x1, waiting for transfers between devices, per_device(): lax.psum_scatter(key_acc, 'row', scatter_dimension=1, tiled=True)  42.2 us
    dot_general x16, matrix products, accumulate(): lax.dot_general(prob_low, columns(grad_all, head_index), contract_first,...  35.7 us
  transfers between devices with their start and end apart: 7, of which 5 were waited for; matrix products, arithmetic and copies ran while one was open for 6% of the time, Pallas kernels for 0%

commit v1 on v0

v1 whole, which is shorter than its diff:
```python
import math

import jax
import jax.numpy as jnp
from jax import lax
from jax.experimental import pallas as pl
from jax.experimental.pallas import tpu as pltpu
from jax.sharding import PartitionSpec as P

HEAD_DIM = 128
BLK = 768
NB = 4
TILE = 512
TILES = NB * BLK // TILE
HALF = NB * BLK // 2
AUG = 144
SCALE = 1.0 / math.sqrt(HEAD_DIM)
LOG2E = math.log2(math.e)
MESH = pl.DeviceIdType.MESH
F32 = jnp.float32
BF16 = jnp.bfloat16


def order(d):
    return jnp.where(d == 2, 3, jnp.where(d == 3, 2, d))


def z_of(p, j):
    return lax.rem(p, 4) if j == 0 else 3 - lax.rem(p, 4)


def dot(a, b):
    return jnp.dot(a, b, preferred_element_type=F32)


def dot_nt(a, b):
    return lax.dot_general(a, b, (((1,), (1,)), ((), ())), preferred_element_type=F32)


def kernel(
    q_in, k_in, v_in, g_in,
    dq_rx, dk_rx, dv_rx,
    kb, vb, xr, via, qgb, kt, vt, qt, gt, qft, gft,
    s0, s1, prob, ot, stat_tx, stat_rx, rows, dqt, dk_acc, dv_acc,
    dq_tx, sib_tx, sib_rx, kv_tx,
    k_rs, v_rs, xr_rs, via_rs, qg_rs, st_rs, sib_rs, dq_rs, kv_rs,
    home_ss, xr_ss, self_s, fwd_ss, hop_ss, st_ss, sib_ss, dq_ss, kv_ss,
):
    r, col, g = lax.axis_index("row"), lax.axis_index("col"), lax.axis_index("head")
    y, c = r // 2, lax.rem(r, 2)
    xh, z = col // 4, lax.rem(col, 4)
    low = lax.rem(2 * y, 4)
    first = jnp.logical_and(z >= low, z < low + 2)
    pw = jnp.where(first, 2 * y + z - low, 2 * y + 3 - z - low)
    jw = jnp.where(first, 0, 1)
    aw = lax.rem(pw, 2)
    pk, pq = r, col
    partner = (y, c, 1 - xh, z)
    sibling = (y, 1 - c, xh, z)
    relay = c == aw

    up, down = lax.rem(xh + g, 2), lax.rem(xh + 1 - g, 2)

    def dev(t):
        yy, cc, xx, zz = t[:4]
        return (2 * yy + cc, 4 * xx + zz, g if len(t) == 4 else t[4])

    def is_me(t):
        yy, cc, xx, zz = t
        return jnp.logical_and(2 * yy + cc == r, 4 * xx + zz == col)

    barrier = pltpu.get_barrier_semaphore()
    greeted = [partner, sibling] + [(y, c, xx, zz, 1 - g) for xx in (up, down) for zz in (z, 3 - z)]
    greeted += [(lax.rem(y + d, 4), c, xh, z) for d in (1, 2, 3)]
    greeted += [(y, cc, xh, lax.rem(z + d, 4)) for d in (1, 2, 3) for cc in range(2)]
    greeted += [(lax.rem(y + d, 4), c, pw // 4, lax.rem(pw, 4)) for d in range(4)]
    greeted += [(pq // 2, c, xx, z_of(pq, j)) for j in range(2) for xx in range(2)]
    for t in greeted:
        pl.semaphore_signal(barrier, inc=1, device_id=dev(t), device_id_type=MESH)
    pl.semaphore_wait(barrier, len(greeted))

    def remote(src, dst, t, ssem, rsem):
        return pltpu.make_async_remote_copy(
            src_ref=src, dst_ref=dst, send_sem=ssem, recv_sem=rsem, device_id=dev(t), device_id_type=MESH
        )

    def put(src, dst, t, ssem, rsem):
        me = is_me(t)

        @pl.when(jnp.logical_not(me))
        def _():
            remote(src, dst, t, ssem, rsem).start()

        @pl.when(me)
        def _():
            pltpu.make_async_copy(src, dst, rsem).start()

    def sent(src, dst, t, ssem, rsem):
        @pl.when(jnp.logical_not(is_me(t)))
        def _():
            remote(src, dst, t, ssem, rsem).wait_send()

    def arrived(dst, rsem):
        pltpu.make_async_copy(dst, dst, rsem).wait()

    def cols(j):
        return pl.ds(j * HEAD_DIM, HEAD_DIM)

    def spread(arr, ref):
        slot = pq // 2
        pltpu.make_async_copy(ref.at[:, cols(0)], via.at[arr, slot], via_rs.at[arr, slot]).start()
        out = []
        for n, (j, t) in enumerate(((0, (y, c, up, z, 1 - g)), (1, (y, c, down, z, 1 - g)))):
            out.append(remote(ref.at[:, cols(j)], xr.at[arr, n], t, home_ss.at[arr, n], xr_rs.at[arr, n]))
        t = (y, c, xh, 3 - z)
        out.append(remote(ref.at[:, cols(1)], via.at[arr, slot], t, home_ss.at[arr, 2], via_rs.at[arr, slot]))
        for copy in out:
            copy.start()
        return out

    def cross(arr):
        out = []
        for n, (origin, to) in enumerate(((down, (y, c, up, z, 1 - g)), (up, (y, c, down, 3 - z, 1 - g)))):
            slot = (4 * origin + z) // 2
            arrived(xr.at[arr, n], xr_rs.at[arr, n])
            out.append(remote(xr.at[arr, n], via.at[arr, slot], to, xr_ss.at[arr, n], via_rs.at[arr, slot]))
            out[-1].start()
        return out

    def hop(arr):
        out = []
        for n, d in enumerate((1, 3, 2)):
            to = lax.rem(y + d, 4)
            slot = {3: 1, 1: 2, 2: 3}[d]
            arrived(via.at[arr, to], via_rs.at[arr, to])
            out.append(
                remote(via.at[arr, to], qgb.at[arr, slot - 1], (to, c, xh, z), hop_ss.at[arr, n], qg_rs.at[arr, slot - 1])
            )
            out[-1].start()
        return out

    def home_kv(arr, j):
        ref, buf, sem = ((k_in, kb, k_rs), (v_in, vb, v_rs))[arr]
        zz = z_of(pk, j)
        slot = order(lax.rem(z - zz + 4, 4))
        return (ref.at[:, cols(j)], buf.at[slot], (y, c, xh, zz), self_s.at[arr, j], sem.at[slot])

    def forward_kv(arr, n):
        buf, sem = ((kb, k_rs), (vb, v_rs))[arr]
        return remote(buf.at[n], buf.at[n], sibling, fwd_ss.at[arr, n], sem.at[n])

    def span(at, size=TILE):
        return slice(at * size, (at + 1) * size)

    pending = spread(0, q_in)
    for j in range(2):
        put(*home_kv(0, j))
    pending += cross(0)
    arrived(via.at[0, y], via_rs.at[0, y])
    pending += hop(0)
    for j in range(2):
        put(*home_kv(1, j))
    qt[:, span(0, BLK)] = via[0, y].T

    sbuf = (s0, s1)

    def scores(i, n, mx):
        s = dot(kb[n], qt[:, span(i)])
        sbuf[i % 2][n] = s
        return jnp.maximum(mx, jnp.max(s.reshape(BLK // 8, 8, TILE), axis=0))

    lowest = jnp.full((8, TILE), -jnp.inf, F32)

    def first_scores(n, mx):
        arrived(kb.at[n], k_rs.at[n])

        @pl.when(relay)
        def _():
            forward_kv(0, n).start()

        kt[n] = kb[n].T
        return scores(0, n, mx)

    mx = lax.fori_loop(0, NB, first_scores, lowest)
    pending += spread(1, g_in)

    def fetch_v(n, carry):
        arrived(vb.at[n], v_rs.at[n])

        @pl.when(relay)
        def _():
            forward_kv(1, n).start()

        vt[n, :HEAD_DIM, :] = vb[n].T
        vt[n, HEAD_DIM:, :] = jnp.ones((AUG - HEAD_DIM, BLK), BF16)
        return carry

    lax.fori_loop(0, NB, fetch_v, 0)

    def weigh(i, n, m):
        p = jnp.exp2((sbuf[i % 2][n] - m) * (SCALE * LOG2E)).astype(BF16)
        prob[i, n] = p
        ot[:, span(i)] += dot(vt[n], p)

    def stat_copy(half):
        return remote(stat_tx.at[half], stat_rx.at[half], partner, st_ss.at[half], st_rs.at[half])

    def finish(half):
        for b in (2 * half, 2 * half + 1):
            if b == 0:
                arrived(via.at[1, y], via_rs.at[1, y])
                gt[:, span(0, BLK)] = via[1, y].T
            else:
                arrived(qgb.at[1, b - 1], qg_rs.at[1, b - 1])
                gt[:, span(b, BLK)] = qgb[1, b - 1].T
        here = span(half, HALF)
        stat_tx[half, 1:2] = ot[HEAD_DIM : HEAD_DIM + 1, here]
        stat_tx[half, 2:3] = jnp.sum(gt[:, here].astype(F32) * ot[:HEAD_DIM, here], axis=0, keepdims=True)
        stat_copy(half).start()

    ot[...] = jnp.zeros_like(ot)
    for i in range(TILES):
        m = jnp.max(mx, axis=0, keepdims=True)
        stat_tx[i // 3, 0:1, span(i % 3)] = m
        more = i + 1 < TILES
        if i in (0, 2, 3):
            b = max(i, 1)
            arrived(qgb.at[0, b - 1], qg_rs.at[0, b - 1])
            qt[:, span(b, BLK)] = qgb[0, b - 1].T

        def step(n, mx2):
            if more:
                mx2 = scores(i + 1, n, mx2)
            weigh(i, n, m)
            return mx2

        mx = lax.fori_loop(0, NB, step, lowest)
        if i == 0:
            pending += cross(1)
        if i == 1:
            pending += hop(1)
        if i == TILES - 2:
            finish(0)
    finish(1)

    def combine(half):
        stat_copy(half).wait()
        m0, l0, d0 = stat_tx[half, 0:1], stat_tx[half, 1:2], stat_tx[half, 2:3]
        m1, l1, d1 = stat_rx[half, 0:1], stat_rx[half, 1:2], stat_rx[half, 2:3]
        m = jnp.maximum(m0, m1)
        e0 = jnp.exp2((m0 - m) * (SCALE * LOG2E))
        e1 = jnp.exp2((m1 - m) * (SCALE * LOG2E))
        inv = 1.0 / (l0 * e0 + l1 * e1)
        f = e0 * inv
        here = span(half, HALF)
        rows[0:1, here] = (d0 * e0 + d1 * e1) * inv
        rows[1:2, here] = f * SCALE
        gft[:, here] = (gt[:, here].astype(F32) * f).astype(BF16)
        qft[:, here] = (qt[:, here].astype(F32) * (f * SCALE)).astype(BF16)

    dqt[...] = jnp.zeros_like(dqt)
    dk_acc[...] = jnp.zeros_like(dk_acc)
    dv_acc[...] = jnp.zeros_like(dv_acc)

    def dq_args(i):
        t = (lax.rem(y + order(i), 4), c, pw // 4, lax.rem(pw, 4))
        return (dq_tx.at[i], dq_rx.at[jw, xh], t, dq_ss.at[i], dq_rs.at[jw, xh])

    def sib_copy(n):
        return remote(sib_tx.at[n], sib_rx.at[n], sibling, sib_ss.at[n], sib_rs.at[n])

    def kv_args(n, raw):
        t = (y, aw, xh, lax.rem(z + order(n), 4))
        return [(kv_tx.at[n], raw.at[:, cols(j)], t, kv_ss.at[n], kv_rs.at[c, j]) for j in range(2)]

    def by_core(run):
        @pl.when(c == 0)
        def _():
            run(dk_acc, dv_acc, dk_rx)

        @pl.when(c == 1)
        def _():
            run(dv_acc, dk_acc, dv_rx)

    def by_member(run):
        for j in range(2):

            @pl.when(jw == j)
            def _():
                run(j)

    def trade_kv(n):
        def run(_, other, __):
            sib_tx[n] = other[n].astype(BF16)

        by_core(run)
        sib_copy(n).start()

    def reduce_kv(n):
        arrived(sib_rx.at[n], sib_rs.at[n])

        def run(own, _, raw):
            kv_tx[n] = (own[n] + sib_rx[n].astype(F32)).astype(BF16)
            by_member(lambda j: put(*kv_args(n, raw)[j]))

        by_core(run)

    def backward(i, n):
        here = span(i)
        p = prob[i, n]
        dp = dot(vb[n], gt[:, here])
        ds = (p.astype(F32) * (dp - rows[0:1, here])).astype(BF16)
        dv_acc[n] += dot_nt(p, gft[:, here])
        dk_acc[n] += dot_nt(ds, qft[:, here])
        dqt[:, here] += dot(kt[n], ds)

    def send_dq(b):
        here = span(b, BLK)
        dq_tx[b] = (dqt[:, here] * rows[1:2, here]).T.astype(BF16)
        put(*dq_args(b))

    def loop(lo, hi, body):
        def run(n, carry):
            body(n)
            return carry

        lax.fori_loop(lo, hi, run, 0)

    def first_half(n):
        for i in range(3):
            backward(i, n)

    combine(0)
    loop(0, NB, first_half)
    send_dq(0)
    send_dq(1)
    combine(1)

    def second_half(n):
        for i in range(3, 6):
            backward(i, n)
        trade_kv(n)

    loop(0, 2, second_half)
    reduce_kv(jnp.int32(0))

    def most(n):
        for i in range(3, 5):
            backward(i, n)

    loop(2, 4, most)
    send_dq(2)
    reduce_kv(jnp.int32(1))

    def final(n):
        backward(5, n)
        trade_kv(n)

    loop(2, 4, final)
    reduce_kv(jnp.int32(2))
    send_dq(3)
    reduce_kv(jnp.int32(3))

    for j in range(2):
        for n in range(2):
            arrived(dq_rx.at[j, n], dq_rs.at[j, n])
        for arr, raw in ((0, dk_rx), (1, dv_rx)):
            arrived(raw.at[:, cols(j)], kv_rs.at[arr, j])

    for copy in pending:
        copy.wait_send()
    for arr in range(2):
        for j in range(2):
            sent(*home_kv(arr, j))

    @pl.when(relay)
    def _():
        for arr in range(2):
            for n in range(NB):
                forward_kv(arr, n).wait_send()

    for i in range(NB):
        sent(*dq_args(jnp.int32(i)))
        sent(*kv_args(jnp.int32(i), dk_rx)[0])
        sib_copy(i).wait_send()


def collect(dq_raw, dk_raw, dv_raw, dq_out, dk_out, dv_out):
    for j in range(2):
        total = dq_raw[j, 0].astype(F32) + dq_raw[j, 1].astype(F32)
        dq_out[:, j * HEAD_DIM : (j + 1) * HEAD_DIM] = total.astype(BF16)
    dk_out[...] = dk_raw[...]
    dv_out[...] = dv_raw[...]


def per_device(queries, key_states, value_states, out_grad):
    rows, width = queries.shape
    shape = jax.ShapeDtypeStruct((rows, width), BF16)
    vm = pltpu.VMEM
    dma = pltpu.SemaphoreType.DMA
    tile = (NB, BLK, HEAD_DIM)
    tile_t = (NB, HEAD_DIM, BLK)
    flat_t = (HEAD_DIM, NB * BLK)
    flops = 6 * 2 * (NB * BLK) ** 2 * HEAD_DIM
    raw = pl.pallas_call(
        kernel,
        out_shape=(jax.ShapeDtypeStruct((2, 2, BLK, HEAD_DIM), BF16), shape, shape),
        in_specs=[pl.BlockSpec(memory_space=pl.ANY)] * 4,
        out_specs=tuple([pl.BlockSpec(memory_space=pl.ANY)] * 3),
        scratch_shapes=[
            vm(tile, BF16), vm(tile, BF16), vm((2, 2, BLK, HEAD_DIM), BF16), vm((2,) + tile, BF16), vm((2, NB - 1, BLK, HEAD_DIM), BF16),
            vm(tile_t, BF16), vm((NB, AUG, BLK), BF16), vm(flat_t, BF16), vm(flat_t, BF16), vm(flat_t, BF16), vm(flat_t, BF16),
            vm((NB, BLK, TILE), F32), vm((NB, BLK, TILE), F32), vm((TILES, NB, BLK, TILE), BF16), vm((AUG, NB * BLK), F32),
            vm((2, 8, HALF), F32), vm((2, 8, HALF), F32), vm((8, NB * BLK), F32), vm(flat_t, F32),
            vm(tile, F32), vm(tile, F32),
            vm(tile, BF16), vm(tile, BF16), vm(tile, BF16), vm(tile, BF16),
            dma((NB,)), dma((NB,)), dma((2, 2)), dma((2, NB)), dma((2, NB - 1)), dma((NB,)), dma((NB,)), dma((2, 2)), dma((2, 2)),
            dma((2, 3)), dma((2, 2)), dma((2, 2)), dma((2, NB)), dma((2, 3)), dma((NB,)), dma((NB,)), dma((NB,)), dma((NB,)),
        ],
        compiler_params=pltpu.CompilerParams(
            collective_id=0, has_side_effects=True, vmem_limit_bytes=62 * 1024 * 1024
        ),
        cost_estimate=pl.CostEstimate(flops=flops, bytes_accessed=4 * rows * width * 2, transcendentals=(NB * BLK) ** 2),
    )(queries, key_states, value_states, out_grad)
    part = rows // 3
    whole = pl.BlockSpec((part, width), lambda n: (n, 0))
    return pl.pallas_call(
        collect,
        out_shape=(shape, shape, shape),
        grid=(3,),
        in_specs=[pl.BlockSpec((2, 2, part, HEAD_DIM), lambda n: (0, 0, n, 0))] + [whole] * 2,
        out_specs=(whole,) * 3,
    )(*raw)


def solution(mesh):
    placed = (
        P("row", ("head", "col")),
        P("col", ("head", "row")),
        P("col", ("head", "row")),
        P("row", ("head", "col")),
    )
    return jax.shard_map(
        per_device,
        mesh=mesh,
        in_specs=placed,
        out_specs=(P("row", ("head", "col")), P("col", ("head", "row")), P("col", ("head", "row"))),
        check_vma=False,
    )
```

time: 754 us -> 92.9 us (0.12)
  the two profiles are of different devices: /device:TPU:3 before, /device:TPU:24 now
where the time goes in v1:
time: 92.9 us; the launch traced here: 92.7 us
  Pallas kernels  92.1 us (99%)
    pallas_call x1, Pallas kernels, per_device(): pl.pallas_call(kernel, out_shape=(jax.ShapeDtypeStruct((2, 2, BLK, HEAD_D...  88.9 us
    pallas_call x1, Pallas kernels, per_device(): pl.pallas_call(collect, out_shape=(shape, shape, shape), grid=(3,), in_sp...  3.22 us

profile of v1, /device:TPU:24, one launch (start us, length us, event | category | flops | bytes accessed | tf_op | source)
XLA Modules:
  0.0 92.7 jit_solution(4448302817406892621)
XLA Ops:
  0.6 88.9 %shard_map.67 = (bf16[2,2,768,128]{3,2,1,0:T(8,128)(2,1)}, bf16[768,256]{1,0:T(8,128)(2,1)}, bf16[768,256]{1,0:T(8,128)(2,1)}) custom-call(bf16[768,256]{1,0:T(8,128)(2,1)} %q_in.1, bf16[768,256]{1,0:T(8,128)(2,1)} %k_in.1, bf16[768,256]{1,0:T(8,128)(2,1)} %v_in.1, bf16[768,256]{1,0:T(8,128)(2,1)} %g_in.1), custom_call_target="tpu_custom_call" | custom-call | flops 14495514624 | bytes 1572864 | tf_op jit(solution)/shard_map/pallas_call | solution.py:405
  89.5 3.2 %shard_map.68 = (bf16[768,256]{1,0:T(8,128)(2,1)}, bf16[768,256]{1,0:T(8,128)(2,1)}, bf16[768,256]{1,0:T(8,128)(2,1)}) custom-call(bf16[2,2,768,128]{3,2,1,0:T(8,128)(2,1)} %get-tuple-element.6.dq_raw, bf16[768,256]{1,0:T(8,128)(2,1)} %get-tuple-element.7.dk_raw, bf16[768,256]{1,0:T(8,128)(2,1)} %get-tuple-element.8.dv_raw), custom_call_target="tpu_custom_call" | custom-call | tf_op jit(solution)/shard_map/pallas_call | solution.py:427

commit v2 on v1

v2 whole, which is shorter than its diff:
```python
import math

import jax
import jax.numpy as jnp
from jax import lax
from jax.experimental import pallas as pl
from jax.experimental.pallas import tpu as pltpu
from jax.sharding import PartitionSpec as P

HEAD_DIM = 128
BLK = 768
NB = 4
AUG = 144
SCALE = 1.0 / math.sqrt(HEAD_DIM)
LOG2E = math.log2(math.e)
MESH = pl.DeviceIdType.MESH
F32 = jnp.float32
BF16 = jnp.bfloat16


def order(d):
    return jnp.where(d == 2, 3, jnp.where(d == 3, 2, d))


def y_of(p, j):
    return lax.rem(p // 2 + j, 4)


def dot(a, b):
    return jnp.dot(a, b, preferred_element_type=F32)


def dot_nt(a, b):
    return lax.dot_general(a, b, (((1,), (1,)), ((), ())), preferred_element_type=F32)


def kernel(
    q_in, k_in, v_in, g_in,
    dq_rx, dk_rx, dv_rx,
    kb, vb, xr, via, qgb, kt, vt, qt, gt, qft, gft,
    s0, s1, prob, ot, stat_tx, stat_rx, rows, dqt, dk_acc, dv_acc,
    dq_tx, sib_tx, sib_rx, kv_tx, yr,
    k_rs, v_rs, xr_rs, via_rs, qg_rs, st_rs, sib_rs, dq_rs, kv_rs, yr_rs,
    home_ss, xr_ss, self_s, fwd_ss, hop_ss, st_ss, sib_ss, dq_ss, kv_ss, yr_ss,
):
    r, col, g = lax.axis_index("row"), lax.axis_index("col"), lax.axis_index("head")
    y, c = r // 2, lax.rem(r, 2)
    xh, z = col // 4, lax.rem(col, 4)
    jw = lax.rem(y + z // 2, 2)
    pw = z + 4 * (lax.rem(y - jw + 4, 4) // 2)
    aw = lax.rem(pw, 2)
    pk, pq = r, col
    partner = (y, c, 1 - xh, z)
    sibling = (y, 1 - c, xh, z)
    relay = c == aw

    up, down = lax.rem(xh + g, 2), lax.rem(xh + 1 - g, 2)

    def dev(t):
        yy, cc, xx, zz = t[:4]
        return (2 * yy + cc, 4 * xx + zz, g if len(t) == 4 else t[4])

    def is_me(t):
        yy, cc, xx, zz = t
        return jnp.logical_and(2 * yy + cc == r, 4 * xx + zz == col)

    barrier = pltpu.get_barrier_semaphore()
    greeted = [partner, sibling] + [(y, c, xx, z, 1 - g) for xx in (up, down)]
    greeted += [(lax.rem(y + d, 4), c, xh, z) for d in (1, 2, 3)]
    greeted += [(y_of(pk, j), cc, xh, lax.rem(pk, 4)) for j in range(2) for cc in range(2)]
    greeted += [(pw // 2, aw, xh, lax.rem(z + d, 4)) for d in range(4)]
    greeted += [(y, cc, xh, lax.rem(z + d, 4)) for d in (1, 2, 3) for cc in range(2)]
    greeted += [(lax.rem(y + d, 4), c, pw // 4, lax.rem(pw, 4)) for d in range(4)]
    greeted += [(y_of(pq, j), c, xx, z) for j in range(2) for xx in range(2)]
    for t in greeted:
        pl.semaphore_signal(barrier, inc=1, device_id=dev(t), device_id_type=MESH)
    pl.semaphore_wait(barrier, len(greeted))

    def remote(src, dst, t, ssem, rsem):
        return pltpu.make_async_remote_copy(
            src_ref=src, dst_ref=dst, send_sem=ssem, recv_sem=rsem, device_id=dev(t), device_id_type=MESH
        )

    def put(src, dst, t, ssem, rsem):
        me = is_me(t)

        @pl.when(jnp.logical_not(me))
        def _():
            remote(src, dst, t, ssem, rsem).start()

        @pl.when(me)
        def _():
            pltpu.make_async_copy(src, dst, rsem).start()

    def sent(src, dst, t, ssem, rsem):
        @pl.when(jnp.logical_not(is_me(t)))
        def _():
            remote(src, dst, t, ssem, rsem).wait_send()

    def arrived(dst, rsem):
        pltpu.make_async_copy(dst, dst, rsem).wait()

    def cols(j):
        return pl.ds(j * HEAD_DIM, HEAD_DIM)

    def spread(arr, ref):
        out = []
        for j, xx in enumerate((up, down)):
            slot = y_of(pq, j)
            pltpu.make_async_copy(ref.at[:, cols(j)], via.at[arr, slot], via_rs.at[arr, slot]).start()
            t = (y, c, xx, z, 1 - g)
            out.append(remote(ref.at[:, cols(j)], xr.at[arr, j], t, home_ss.at[arr, j], xr_rs.at[arr, j]))
            out[-1].start()
        return out

    def cross(arr):
        out = []
        for j, (origin, xx) in enumerate(((down, up), (up, down))):
            slot = y_of(4 * origin + z, j)
            arrived(xr.at[arr, j], xr_rs.at[arr, j])
            out.append(
                remote(xr.at[arr, j], via.at[arr, slot], (y, c, xx, z, 1 - g), xr_ss.at[arr, j], via_rs.at[arr, slot])
            )
            out[-1].start()
        return out

    def hop(arr):
        out = []
        for n, d in enumerate((1, 3, 2)):
            to = lax.rem(y + d, 4)
            slot = {3: 1, 1: 2, 2: 3}[d]
            arrived(via.at[arr, to], via_rs.at[arr, to])
            out.append(
                remote(via.at[arr, to], qgb.at[arr, slot - 1], (to, c, xh, z), hop_ss.at[arr, n], qg_rs.at[arr, slot - 1])
            )
            out[-1].start()
        return out

    def home_kv(arr, j):
        ref, buf, sem = ((k_in, kb, k_rs), (v_in, vb, v_rs))[arr]
        slot = order(lax.rem(z - lax.rem(pk, 4) + 4, 4))
        t = (y_of(pk, j), c, xh, lax.rem(pk, 4))
        return (ref.at[:, cols(j)], buf.at[slot], t, self_s.at[arr, j], sem.at[slot])

    def forward_kv(arr, n):
        buf, sem = ((kb, k_rs), (vb, v_rs))[arr]
        return remote(buf.at[n], buf.at[n], sibling, fwd_ss.at[arr, n], sem.at[n])

    pending = spread(0, q_in)
    for arr in range(2):
        for j in range(2):
            put(*home_kv(arr, j))
    pending += spread(1, g_in)
    pending += cross(0)
    arrived(via.at[0, y], via_rs.at[0, y])
    qt[0] = via[0, y].T
    pending += hop(0)

    sbuf = (s0, s1)

    def scores(i, n, buf, m):
        s = dot(kb[n], qt[i])
        sbuf[buf][n] = s
        return jnp.maximum(m, jnp.max(s.reshape(BLK // 8, 8, BLK), axis=0))

    lowest = jnp.full((8, BLK), -jnp.inf, F32)
    def first_scores(n, m):
        arrived(kb.at[n], k_rs.at[n])

        @pl.when(relay)
        def _():
            forward_kv(0, n).start()

        kt[n] = kb[n].T
        return scores(0, n, 0, m)

    mx = lax.fori_loop(0, NB, first_scores, lowest)

    def fetch_v(n, carry):
        arrived(vb.at[n], v_rs.at[n])

        @pl.when(relay)
        def _():
            forward_kv(1, n).start()

        vt[n, :HEAD_DIM, :] = vb[n].T
        vt[n, HEAD_DIM:, :] = jnp.ones((AUG - HEAD_DIM, BLK), BF16)
        return carry

    lax.fori_loop(0, NB, fetch_v, 0)
    pending += cross(1)

    def weigh(i, n, buf, m):
        p = jnp.exp2((sbuf[buf][n] - m) * (SCALE * LOG2E)).astype(BF16)
        prob[i, n] = p
        ot[i] += dot(vt[n], p)

    def stat_copy(i):
        return remote(stat_tx.at[i], stat_rx.at[i], partner, st_ss.at[i], st_rs.at[i])

    def finish(i, m):
        if i == 0:
            arrived(via.at[1, y], via_rs.at[1, y])
            gt[0] = via[1, y].T
        else:
            arrived(qgb.at[1, i - 1], qg_rs.at[1, i - 1])
            gt[i] = qgb[1, i - 1].T
        stat_tx[i, 0:1] = m
        stat_tx[i, 1:2] = ot[i, HEAD_DIM : HEAD_DIM + 1]
        stat_tx[i, 2:3] = jnp.sum(gt[i].astype(F32) * ot[i, :HEAD_DIM], axis=0, keepdims=True)
        stat_copy(i).start()

    def forward(i, mx):
        buf = i % 2
        more = i + 1 < NB
        if more:
            arrived(qgb.at[0, i], qg_rs.at[0, i])
            qt[i + 1] = qgb[0, i].T
        m = jnp.max(mx, axis=0, keepdims=True)
        ot[i] = jnp.zeros((AUG, BLK), F32)

        def step(n, mx2):
            if more:
                mx2 = scores(i + 1, n, 1 - buf, mx2)
            weigh(i, n, buf, m)
            return mx2

        return m, lax.fori_loop(0, NB, step, lowest)

    def combine(i):
        stat_copy(i).wait()
        m0, l0, d0 = stat_tx[i, 0:1], stat_tx[i, 1:2], stat_tx[i, 2:3]
        m1, l1, d1 = stat_rx[i, 0:1], stat_rx[i, 1:2], stat_rx[i, 2:3]
        m = jnp.maximum(m0, m1)
        e0 = jnp.exp2((m0 - m) * (SCALE * LOG2E))
        e1 = jnp.exp2((m1 - m) * (SCALE * LOG2E))
        inv = 1.0 / (l0 * e0 + l1 * e1)
        f = e0 * inv
        rows[i, 0:1] = (d0 * e0 + d1 * e1) * inv
        rows[i, 1:2] = f * SCALE
        gft[i] = (gt[i].astype(F32) * f).astype(BF16)
        qft[i] = (qt[i].astype(F32) * (f * SCALE)).astype(BF16)
        dqt[i] = jnp.zeros((HEAD_DIM, BLK), F32)

    dk_acc[...] = jnp.zeros_like(dk_acc)
    dv_acc[...] = jnp.zeros_like(dv_acc)

    def dq_args(i):
        t = (lax.rem(y + order(i), 4), c, pw // 4, lax.rem(pw, 4))
        return (dq_tx.at[i], dq_rx.at[jw, xh], t, dq_ss.at[i], dq_rs.at[jw, xh])

    def sib_copy(n):
        return remote(sib_tx.at[n], sib_rx.at[n], sibling, sib_ss.at[n], sib_rs.at[n])

    def kv_args(n, raw):
        t = (y, aw, xh, lax.rem(z + order(n), 4))
        return [
            (kv_tx.at[n], raw.at[:, cols(0)], t, kv_ss.at[n], kv_rs.at[c, 0]),
            (kv_tx.at[n], yr.at[c], t, kv_ss.at[n], yr_rs.at[c]),
        ]

    def relay_down(arr):
        raw = (dk_rx, dv_rx)[arr]
        t = (lax.rem(y + 3, 4), c, xh, z)
        return remote(yr.at[arr], raw.at[:, cols(1)], t, yr_ss.at[arr], kv_rs.at[arr, 1])

    def by_core(run):
        @pl.when(c == 0)
        def _():
            run(dk_acc, dv_acc, dk_rx)

        @pl.when(c == 1)
        def _():
            run(dv_acc, dk_acc, dv_rx)

    def by_member(run):
        for j in range(2):

            @pl.when(jw == j)
            def _():
                run(j)

    def trade_kv(n):
        def run(_, other, __):
            sib_tx[n] = other[n].astype(BF16)

        by_core(run)
        sib_copy(n).start()

    def reduce_kv(n):
        arrived(sib_rx.at[n], sib_rs.at[n])

        def run(own, _, raw):
            kv_tx[n] = (own[n] + sib_rx[n].astype(F32)).astype(BF16)
            by_member(lambda j: put(*kv_args(n, raw)[j]))

        by_core(run)

    def backward(i, n):
        p = prob[i, n]
        dp = dot(vb[n], gt[i])
        ds = (p.astype(F32) * (dp - rows[i, 0:1])).astype(BF16)
        dv_acc[n] += dot_nt(p, gft[i])
        dk_acc[n] += dot_nt(ds, qft[i])
        dqt[i] += dot(kt[n], ds)

    def send_dq(i):
        dq_tx[i] = (dqt[i] * rows[i, 1:2]).T.astype(BF16)
        put(*dq_args(i))

    def loop(lo, hi, body):
        def run(n, carry):
            body(n)
            return carry

        lax.fori_loop(lo, hi, run, 0)

    peaks = []
    for i in range(NB):
        m, mx = forward(i, mx)
        peaks.append(m)
        if i == 0:
            pending += hop(1)
        if i == 2:
            finish(0, peaks[0])
            finish(1, peaks[1])
    finish(2, peaks[2])
    finish(3, peaks[3])

    def early(i):
        def pair(n):
            backward(i, 2 * n)
            backward(i, 2 * n + 1)

        combine(i)
        loop(0, NB // 2, pair)
        send_dq(i)

    early(1)
    early(3)
    combine(2)
    combine(0)

    def both(n):
        backward(2, n)
        backward(0, n)
        trade_kv(n)

    loop(0, 2, both)
    reduce_kv(jnp.int32(0))
    backward(2, 2)
    backward(2, 3)
    send_dq(2)
    reduce_kv(jnp.int32(1))

    def final(n):
        backward(0, n)
        trade_kv(n)

    loop(2, 4, final)
    reduce_kv(jnp.int32(2))
    send_dq(0)
    reduce_kv(jnp.int32(3))
    for arr in range(2):
        arrived(yr.at[arr], yr_rs.at[arr])
        relay_down(arr).start()

    for j in range(2):
        for n in range(2):
            arrived(dq_rx.at[j, n], dq_rs.at[j, n])
        for arr, raw in ((0, dk_rx), (1, dv_rx)):
            arrived(raw.at[:, cols(j)], kv_rs.at[arr, j])

    for copy in pending:
        copy.wait_send()
    for arr in range(2):
        for j in range(2):
            sent(*home_kv(arr, j))

    @pl.when(relay)
    def _():
        for arr in range(2):
            for n in range(NB):
                forward_kv(arr, n).wait_send()

    for i in range(NB):
        sent(*dq_args(jnp.int32(i)))
        sent(*kv_args(jnp.int32(i), dk_rx)[0])
        sib_copy(i).wait_send()
    for arr in range(2):
        relay_down(arr).wait_send()


def collect(dq_raw, dk_raw, dv_raw, dq_out, dk_out, dv_out):
    for j in range(2):
        total = dq_raw[j, 0].astype(F32) + dq_raw[j, 1].astype(F32)
        dq_out[:, j * HEAD_DIM : (j + 1) * HEAD_DIM] = total.astype(BF16)
    dk_out[...] = dk_raw[...]
    dv_out[...] = dv_raw[...]


def per_device(queries, key_states, value_states, out_grad):
    rows, width = queries.shape
    shape = jax.ShapeDtypeStruct((rows, width), BF16)
    vm = pltpu.VMEM
    dma = pltpu.SemaphoreType.DMA
    tile = (NB, BLK, HEAD_DIM)
    tile_t = (NB, HEAD_DIM, BLK)
    flops = 6 * 2 * (NB * BLK) ** 2 * HEAD_DIM
    raw = pl.pallas_call(
        kernel,
        out_shape=(jax.ShapeDtypeStruct((2, 2, BLK, HEAD_DIM), BF16), shape, shape),
        in_specs=[pl.BlockSpec(memory_space=pl.ANY)] * 4,
        out_specs=tuple([pl.BlockSpec(memory_space=pl.ANY)] * 3),
        scratch_shapes=[
            vm(tile, BF16), vm(tile, BF16), vm((2, 2, BLK, HEAD_DIM), BF16), vm((2,) + tile, BF16), vm((2, NB - 1, BLK, HEAD_DIM), BF16),
            vm(tile_t, BF16), vm((NB, AUG, BLK), BF16), vm(tile_t, BF16), vm(tile_t, BF16),
            vm(tile_t, BF16), vm(tile_t, BF16),
            vm((NB, BLK, BLK), F32), vm((NB, BLK, BLK), F32), vm((NB, NB, BLK, BLK), BF16), vm((NB, AUG, BLK), F32),
            vm((NB, 8, BLK), F32), vm((NB, 8, BLK), F32), vm((NB, 8, BLK), F32), vm(tile_t, F32),
            vm(tile, F32), vm(tile, F32),
            vm(tile, BF16), vm(tile, BF16), vm(tile, BF16), vm(tile, BF16), vm((2, BLK, HEAD_DIM), BF16),
            dma((NB,)), dma((NB,)), dma((2, 2)), dma((2, NB)), dma((2, NB - 1)), dma((NB,)), dma((NB,)), dma((2, 2)), dma((2, 2)), dma((2,)),
            dma((2, 2)), dma((2, 2)), dma((2, 2)), dma((2, NB)), dma((2, 3)), dma((NB,)), dma((NB,)), dma((NB,)), dma((NB,)), dma((2,)),
        ],
        compiler_params=pltpu.CompilerParams(
            collective_id=0, has_side_effects=True, vmem_limit_bytes=62 * 1024 * 1024
        ),
        cost_estimate=pl.CostEstimate(flops=flops, bytes_accessed=4 * rows * width * 2, transcendentals=(NB * BLK) ** 2),
    )(queries, key_states, value_states, out_grad)
    part = rows // 3
    whole = pl.BlockSpec((part, width), lambda n: (n, 0))
    return pl.pallas_call(
        collect,
        out_shape=(shape, shape, shape),
        grid=(3,),
        in_specs=[pl.BlockSpec((2, 2, part, HEAD_DIM), lambda n: (0, 0, n, 0))] + [whole] * 2,
        out_specs=(whole,) * 3,
    )(*raw)


def solution(mesh):
    placed = (
        P("row", ("head", "col")),
        P("col", ("head", "row")),
        P("col", ("head", "row")),
        P("row", ("head", "col")),
    )
    return jax.shard_map(
        per_device,
        mesh=mesh,
        in_specs=placed,
        out_specs=(P("row", ("head", "col")), P("col", ("head", "row")), P("col", ("head", "row"))),
        check_vma=False,
    )
```

time: 92.9 us -> 88.1 us (0.948)
  the two profiles are of different devices: /device:TPU:24 before, /device:TPU:40 now
where the time goes in v2:
time: 88.1 us; the launch traced here: 87.9 us
  Pallas kernels  87.3 us (99%)
    pallas_call x1, Pallas kernels, per_device(): pl.pallas_call(kernel, out_shape=(jax.ShapeDtypeStruct((2, 2, BLK, HEAD_D...  84.1 us
    pallas_call x1, Pallas kernels, per_device(): pl.pallas_call(collect, out_shape=(shape, shape, shape), grid=(3,), in_sp...  3.22 us

profile of v2, /device:TPU:40, one launch (start us, length us, event | category | flops | bytes accessed | tf_op | source)
XLA Modules:
  0.0 87.9 jit_solution(14075723136027455865)
XLA Ops:
  0.6 84.1 %shard_map.67 = (bf16[2,2,768,128]{3,2,1,0:T(8,128)(2,1)}, bf16[768,256]{1,0:T(8,128)(2,1)}, bf16[768,256]{1,0:T(8,128)(2,1)}) custom-call(bf16[768,256]{1,0:T(8,128)(2,1)} %q_in.1, bf16[768,256]{1,0:T(8,128)(2,1)} %k_in.1, bf16[768,256]{1,0:T(8,128)(2,1)} %v_in.1, bf16[768,256]{1,0:T(8,128)(2,1)} %g_in.1), custom_call_target="tpu_custom_call" | custom-call | flops 14495514624 | bytes 1572864 | tf_op jit(solution)/shard_map/pallas_call | solution.py:410
  84.7 3.2 %shard_map.68 = (bf16[768,256]{1,0:T(8,128)(2,1)}, bf16[768,256]{1,0:T(8,128)(2,1)}, bf16[768,256]{1,0:T(8,128)(2,1)}) custom-call(bf16[2,2,768,128]{3,2,1,0:T(8,128)(2,1)} %get-tuple-element.6.dq_raw, bf16[768,256]{1,0:T(8,128)(2,1)} %get-tuple-element.7.dk_raw, bf16[768,256]{1,0:T(8,128)(2,1)} %get-tuple-element.8.dv_raw), custom_call_target="tpu_custom_call" | custom-call | tf_op jit(solution)/shard_map/pallas_call | solution.py:433

commit v3 on v2

--- a/solution.py
+++ b/solution.py
@@ -336,34 +336,41 @@
         loop(0, NB // 2, pair)
         send_dq(i)
 
-    early(1)
-    early(3)
+    loop(0, 2, lambda t: early(1 + 2 * t))
     combine(2)
     combine(0)
 
-    def both(n):
+    def both(t):
+        n = 3 - 2 * t
         backward(2, n)
         backward(0, n)
         trade_kv(n)
 
+    def relay_now():
+        for arr in range(2):
+            arrived(yr.at[arr], yr_rs.at[arr])
+            relay_down(arr).start()
+
+    passed = order(lax.rem(z - 2 * lax.rem(y + 1, 2) - c + 4, 4))
+
     loop(0, 2, both)
-    reduce_kv(jnp.int32(0))
+    reduce_kv(jnp.int32(3))
     backward(2, 2)
-    backward(2, 3)
+    backward(2, 0)
     send_dq(2)
     reduce_kv(jnp.int32(1))
 
-    def final(n):
+    def final(t):
+        pl.when(passed == 3 - 2 * t)(relay_now)
+        n = 2 - 2 * t
         backward(0, n)
         trade_kv(n)
 
-    loop(2, 4, final)
+    loop(0, 2, final)
     reduce_kv(jnp.int32(2))
     send_dq(0)
-    reduce_kv(jnp.int32(3))
-    for arr in range(2):
-        arrived(yr.at[arr], yr_rs.at[arr])
-        relay_down(arr).start()
+    reduce_kv(jnp.int32(0))
+    pl.when(lax.rem(passed, 2) == 0)(relay_now)
 
     for j in range(2):
         for n in range(2):
@@ -428,13 +435,11 @@
         ),
         cost_estimate=pl.CostEstimate(flops=flops, bytes_accessed=4 * rows * width * 2, transcendentals=(NB * BLK) ** 2),
     )(queries, key_states, value_states, out_grad)
-    part = rows // 3
-    whole = pl.BlockSpec((part, width), lambda n: (n, 0))
+    whole = pl.BlockSpec(memory_space=pltpu.VMEM)
     return pl.pallas_call(
         collect,
         out_shape=(shape, shape, shape),
-        grid=(3,),
-        in_specs=[pl.BlockSpec((2, 2, part, HEAD_DIM), lambda n: (0, 0, n, 0))] + [whole] * 2,
+        in_specs=[whole] * 3,
         out_specs=(whole,) * 3,
     )(*raw)
 

time: 88.1 us -> 85.7 us (0.973)
  the two profiles are of different devices: /device:TPU:40 before, /device:TPU:3 now
where the time goes in v3:
time: 85.7 us; the launch traced here: 85.6 us
  Pallas kernels  84.9 us (99%)
    pallas_call x1, Pallas kernels, per_device(): pl.pallas_call(kernel, out_shape=(jax.ShapeDtypeStruct((2, 2, BLK, HEAD_D...  82.5 us
    pallas_call x1, Pallas kernels, per_device(): pl.pallas_call(collect, out_shape=(shape, shape, shape), in_specs=[whole]...  2.38 us

profile of v3, /device:TPU:3, one launch (start us, length us, event | category | flops | bytes accessed | tf_op | source)
XLA Modules:
  0.0 85.6 jit_solution(13522208634621038570)
XLA Ops:
  0.6 82.5 %shard_map.67 = (bf16[2,2,768,128]{3,2,1,0:T(8,128)(2,1)}, bf16[768,256]{1,0:T(8,128)(2,1)}, bf16[768,256]{1,0:T(8,128)(2,1)}) custom-call(bf16[768,256]{1,0:T(8,128)(2,1)} %q_in.1, bf16[768,256]{1,0:T(8,128)(2,1)} %k_in.1, bf16[768,256]{1,0:T(8,128)(2,1)} %v_in.1, bf16[768,256]{1,0:T(8,128)(2,1)} %g_in.1), custom_call_target="tpu_custom_call" | custom-call | flops 14495514624 | bytes 1572864 | tf_op jit(solution)/shard_map/pallas_call | solution.py:417
  83.2 2.4 %shard_map.68 = (bf16[768,256]{1,0:T(8,128)(2,1)}, bf16[768,256]{1,0:T(8,128)(2,1)}, bf16[768,256]{1,0:T(8,128)(2,1)}) custom-call(bf16[2,2,768,128]{3,2,1,0:T(8,128)(2,1)} %get-tuple-element.6.dq_raw, bf16[768,256]{1,0:T(8,128)(2,1)} %get-tuple-element.7.dk_raw, bf16[768,256]{1,0:T(8,128)(2,1)} %get-tuple-element.8.dv_raw), custom_call_target="tpu_custom_call" | custom-call | tf_op jit(solution)/shard_map/pallas_call | solution.py:439

commit v4 on v3

--- a/solution.py
+++ b/solution.py
@@ -124,17 +124,16 @@
             out[-1].start()
         return out
 
-    def hop(arr):
-        out = []
-        for n, d in enumerate((1, 3, 2)):
-            to = lax.rem(y + d, 4)
-            slot = {3: 1, 1: 2, 2: 3}[d]
-            arrived(via.at[arr, to], via_rs.at[arr, to])
-            out.append(
-                remote(via.at[arr, to], qgb.at[arr, slot - 1], (to, c, xh, z), hop_ss.at[arr, n], qg_rs.at[arr, slot - 1])
-            )
-            out[-1].start()
-        return out
+    def hop_copy(arr, n):
+        d = (1, 3, 2)[n]
+        to = lax.rem(y + d, 4)
+        slot = {3: 1, 1: 2, 2: 3}[d] - 1
+        return remote(via.at[arr, to], qgb.at[arr, slot], (to, c, xh, z), hop_ss.at[arr, n], qg_rs.at[arr, slot])
+
+    def hop(arr, n):
+        to = lax.rem(y + (1, 3, 2)[n], 4)
+        arrived(via.at[arr, to], via_rs.at[arr, to])
+        hop_copy(arr, n).start()
 
     def home_kv(arr, j):
         ref, buf, sem = ((k_in, kb, k_rs), (v_in, vb, v_rs))[arr]
@@ -154,7 +153,9 @@
     pending += cross(0)
     arrived(via.at[0, y], via_rs.at[0, y])
     qt[0] = via[0, y].T
-    pending += hop(0)
+    for n in range(3):
+        hop(0, n)
+    pending += [hop_copy(arr, n) for arr in range(2) for n in range(3)]
 
     sbuf = (s0, s1)
 
@@ -176,7 +177,7 @@
 
     mx = lax.fori_loop(0, NB, first_scores, lowest)
 
-    def fetch_v(n, carry):
+    def fetch_v(n):
         arrived(vb.at[n], v_rs.at[n])
 
         @pl.when(relay)
@@ -185,10 +186,6 @@
 
         vt[n, :HEAD_DIM, :] = vb[n].T
         vt[n, HEAD_DIM:, :] = jnp.ones((AUG - HEAD_DIM, BLK), BF16)
-        return carry
-
-    lax.fori_loop(0, NB, fetch_v, 0)
-    pending += cross(1)
 
     def weigh(i, n, buf, m):
         p = jnp.exp2((sbuf[buf][n] - m) * (SCALE * LOG2E)).astype(BF16)
@@ -220,9 +217,14 @@
         ot[i] = jnp.zeros((AUG, BLK), F32)
 
         def step(n, mx2):
+            if i == 0:
+                fetch_v(n)
             if more:
                 mx2 = scores(i + 1, n, 1 - buf, mx2)
             weigh(i, n, buf, m)
+            if i == 0:
+                for k in range(3):
+                    pl.when(n == k + 1)(lambda: hop(1, k))
             return mx2
 
         return m, lax.fori_loop(0, NB, step, lowest)
@@ -315,12 +317,11 @@
 
         lax.fori_loop(lo, hi, run, 0)
 
+    pending += cross(1)
     peaks = []
     for i in range(NB):
         m, mx = forward(i, mx)
         peaks.append(m)
-        if i == 0:
-            pending += hop(1)
         if i == 2:
             finish(0, peaks[0])
             finish(1, peaks[1])

time: 85.7 us -> 87.9 us (1.026)
  the two profiles are of different devices: /device:TPU:3 before, /device:TPU:1 now
where the time goes in v4:
time: 87.9 us; the launch traced here: 87.8 us
  Pallas kernels  87.1 us (99%)
    pallas_call x1, Pallas kernels, per_device(): pl.pallas_call(kernel, out_shape=(jax.ShapeDtypeStruct((2, 2, BLK, HEAD_D...  84.7 us
    pallas_call x1, Pallas kernels, per_device(): pl.pallas_call(collect, out_shape=(shape, shape, shape), in_specs=[whole]...  2.38 us

profile of v4, /device:TPU:1, one launch (start us, length us, event | category | flops | bytes accessed | tf_op | source)
XLA Modules:
  0.0 87.8 jit_solution(3429788402315194531)
XLA Ops:
  0.6 84.7 %shard_map.67 = (bf16[2,2,768,128]{3,2,1,0:T(8,128)(2,1)}, bf16[768,256]{1,0:T(8,128)(2,1)}, bf16[768,256]{1,0:T(8,128)(2,1)}) custom-call(bf16[768,256]{1,0:T(8,128)(2,1)} %q_in.1, bf16[768,256]{1,0:T(8,128)(2,1)} %k_in.1, bf16[768,256]{1,0:T(8,128)(2,1)} %v_in.1, bf16[768,256]{1,0:T(8,128)(2,1)} %g_in.1), custom_call_target="tpu_custom_call" | custom-call | flops 14495514624 | bytes 1572864 | tf_op jit(solution)/shard_map/pallas_call | solution.py:418
  85.4 2.4 %shard_map.68 = (bf16[768,256]{1,0:T(8,128)(2,1)}, bf16[768,256]{1,0:T(8,128)(2,1)}, bf16[768,256]{1,0:T(8,128)(2,1)}) custom-call(bf16[2,2,768,128]{3,2,1,0:T(8,128)(2,1)} %get-tuple-element.6.dq_raw, bf16[768,256]{1,0:T(8,128)(2,1)} %get-tuple-element.7.dk_raw, bf16[768,256]{1,0:T(8,128)(2,1)} %get-tuple-element.8.dv_raw), custom_call_target="tpu_custom_call" | custom-call | tf_op jit(solution)/shard_map/pallas_call | solution.py:440

commit v5 on v3

--- a/solution.py
+++ b/solution.py
@@ -187,8 +187,9 @@
         vt[n, HEAD_DIM:, :] = jnp.ones((AUG - HEAD_DIM, BLK), BF16)
         return carry
 
+    pending += cross(1)
     lax.fori_loop(0, NB, fetch_v, 0)
-    pending += cross(1)
+    pending += hop(1)
 
     def weigh(i, n, buf, m):
         p = jnp.exp2((sbuf[buf][n] - m) * (SCALE * LOG2E)).astype(BF16)
@@ -319,8 +320,6 @@
     for i in range(NB):
         m, mx = forward(i, mx)
         peaks.append(m)
-        if i == 0:
-            pending += hop(1)
         if i == 2:
             finish(0, peaks[0])
             finish(1, peaks[1])

time: 85.7 us -> 85.6 us (level); the launches traced: 85.6 us -> 84.4 us
  Pallas kernels: 84.9 us -> 83.7 us
    pallas_call x1, Pallas kernels: 82.5 us -> 81.3 us  [per_device(): pl.pallas_call(kernel, out_shape=(jax.ShapeDtypeStruct((2, 2, BLK, HEAD_D...]
where the time goes in v5:
time: 85.6 us; the launch traced here: 84.4 us
  Pallas kernels  83.7 us (98%)
    pallas_call x1, Pallas kernels, per_device(): pl.pallas_call(kernel, out_shape=(jax.ShapeDtypeStruct((2, 2, BLK, HEAD_D...  81.3 us
    pallas_call x1, Pallas kernels, per_device(): pl.pallas_call(collect, out_shape=(shape, shape, shape), in_specs=[whole]...  2.38 us

profile of v5, /device:TPU:3, one launch (start us, length us, event | category | flops | bytes accessed | tf_op | source)
XLA Modules:
  0.0 84.4 jit_solution(7587168545157481564)
XLA Ops:
  0.6 81.3 %shard_map.67 = (bf16[2,2,768,128]{3,2,1,0:T(8,128)(2,1)}, bf16[768,256]{1,0:T(8,128)(2,1)}, bf16[768,256]{1,0:T(8,128)(2,1)}) custom-call(bf16[768,256]{1,0:T(8,128)(2,1)} %q_in.1, bf16[768,256]{1,0:T(8,128)(2,1)} %k_in.1, bf16[768,256]{1,0:T(8,128)(2,1)} %v_in.1, bf16[768,256]{1,0:T(8,128)(2,1)} %g_in.1), custom_call_target="tpu_custom_call" | custom-call | flops 14495514624 | bytes 1572864 | tf_op jit(solution)/shard_map/pallas_call | solution.py:416
  82.0 2.4 %shard_map.68 = (bf16[768,256]{1,0:T(8,128)(2,1)}, bf16[768,256]{1,0:T(8,128)(2,1)}, bf16[768,256]{1,0:T(8,128)(2,1)}) custom-call(bf16[2,2,768,128]{3,2,1,0:T(8,128)(2,1)} %get-tuple-element.6.dq_raw, bf16[768,256]{1,0:T(8,128)(2,1)} %get-tuple-element.7.dk_raw, bf16[768,256]{1,0:T(8,128)(2,1)} %get-tuple-element.8.dv_raw), custom_call_target="tpu_custom_call" | custom-call | tf_op jit(solution)/shard_map/pallas_call | solution.py:438

commit v6 on v3

--- a/solution.py
+++ b/solution.py
@@ -151,6 +151,8 @@
         for j in range(2):
             put(*home_kv(arr, j))
     pending += spread(1, g_in)
+    for total in (dk_acc, dv_acc, dqt, ot):
+        total[...] = jnp.zeros_like(total)
     pending += cross(0)
     arrived(via.at[0, y], via_rs.at[0, y])
     qt[0] = via[0, y].T
@@ -217,15 +219,15 @@
             arrived(qgb.at[0, i], qg_rs.at[0, i])
             qt[i + 1] = qgb[0, i].T
         m = jnp.max(mx, axis=0, keepdims=True)
-        ot[i] = jnp.zeros((AUG, BLK), F32)
-
-        def step(n, mx2):
-            if more:
-                mx2 = scores(i + 1, n, 1 - buf, mx2)
-            weigh(i, n, buf, m)
+
+        def step(at, mx2):
+            for n in (2 * at, 2 * at + 1):
+                if more:
+                    mx2 = scores(i + 1, n, 1 - buf, mx2)
+                weigh(i, n, buf, m)
             return mx2
 
-        return m, lax.fori_loop(0, NB, step, lowest)
+        return m, lax.fori_loop(0, NB // 2, step, lowest)
 
     def combine(i):
         stat_copy(i).wait()
@@ -240,10 +242,7 @@
         rows[i, 1:2] = f * SCALE
         gft[i] = (gt[i].astype(F32) * f).astype(BF16)
         qft[i] = (qt[i].astype(F32) * (f * SCALE)).astype(BF16)
-        dqt[i] = jnp.zeros((HEAD_DIM, BLK), F32)
-
-    dk_acc[...] = jnp.zeros_like(dk_acc)
-    dv_acc[...] = jnp.zeros_like(dv_acc)
+
 
     def dq_args(i):
         t = (lax.rem(y + order(i), 4), c, pw // 4, lax.rem(pw, 4))

time: 85.7 us -> 86.4 us (level)
  no operation moved by 1% of the time
where the time goes in v6:
time: 86.4 us; the launch traced here: 86.2 us
  Pallas kernels  85.6 us (99%)
    pallas_call x1, Pallas kernels, per_device(): pl.pallas_call(kernel, out_shape=(jax.ShapeDtypeStruct((2, 2, BLK, HEAD_D...  83.2 us
    pallas_call x1, Pallas kernels, per_device(): pl.pallas_call(collect, out_shape=(shape, shape, shape), in_specs=[whole]...  2.38 us

profile of v6, /device:TPU:3, one launch (start us, length us, event | category | flops | bytes accessed | tf_op | source)
XLA Modules:
  0.0 86.2 jit_solution(14261607673997263310)
XLA Ops:
  0.6 83.2 %shard_map.67 = (bf16[2,2,768,128]{3,2,1,0:T(8,128)(2,1)}, bf16[768,256]{1,0:T(8,128)(2,1)}, bf16[768,256]{1,0:T(8,128)(2,1)}) custom-call(bf16[768,256]{1,0:T(8,128)(2,1)} %q_in.1, bf16[768,256]{1,0:T(8,128)(2,1)} %k_in.1, bf16[768,256]{1,0:T(8,128)(2,1)} %v_in.1, bf16[768,256]{1,0:T(8,128)(2,1)} %g_in.1), custom_call_target="tpu_custom_call" | custom-call | flops 14495514624 | bytes 1572864 | tf_op jit(solution)/shard_map/pallas_call | solution.py:416
  83.8 2.4 %shard_map.68 = (bf16[768,256]{1,0:T(8,128)(2,1)}, bf16[768,256]{1,0:T(8,128)(2,1)}, bf16[768,256]{1,0:T(8,128)(2,1)}) custom-call(bf16[2,2,768,128]{3,2,1,0:T(8,128)(2,1)} %get-tuple-element.6.dq_raw, bf16[768,256]{1,0:T(8,128)(2,1)} %get-tuple-element.7.dk_raw, bf16[768,256]{1,0:T(8,128)(2,1)} %get-tuple-element.8.dv_raw), custom_call_target="tpu_custom_call" | custom-call | tf_op jit(solution)/shard_map/pallas_call | solution.py:438

commit v7 on v3

--- a/solution.py
+++ b/solution.py
@@ -151,7 +151,20 @@
         for j in range(2):
             put(*home_kv(arr, j))
     pending += spread(1, g_in)
+    for total in (dk_acc, dv_acc, dqt, ot):
+        total[...] = jnp.zeros_like(total)
     pending += cross(0)
+
+    def fetch_k(n, carry):
+        arrived(kb.at[n], k_rs.at[n])
+
+        @pl.when(relay)
+        def _():
+            forward_kv(0, n).start()
+
+        return carry
+
+    lax.fori_loop(0, NB, fetch_k, 0)
     arrived(via.at[0, y], via_rs.at[0, y])
     qt[0] = via[0, y].T
     pending += hop(0)
@@ -165,12 +178,6 @@
 
     lowest = jnp.full((8, BLK), -jnp.inf, F32)
     def first_scores(n, m):
-        arrived(kb.at[n], k_rs.at[n])
-
-        @pl.when(relay)
-        def _():
-            forward_kv(0, n).start()
-
         kt[n] = kb[n].T
         return scores(0, n, 0, m)
 
@@ -217,7 +224,6 @@
             arrived(qgb.at[0, i], qg_rs.at[0, i])
             qt[i + 1] = qgb[0, i].T
         m = jnp.max(mx, axis=0, keepdims=True)
-        ot[i] = jnp.zeros((AUG, BLK), F32)
 
         def step(n, mx2):
             if more:
@@ -240,10 +246,7 @@
         rows[i, 1:2] = f * SCALE
         gft[i] = (gt[i].astype(F32) * f).astype(BF16)
         qft[i] = (qt[i].astype(F32) * (f * SCALE)).astype(BF16)
-        dqt[i] = jnp.zeros((HEAD_DIM, BLK), F32)
-
-    dk_acc[...] = jnp.zeros_like(dk_acc)
-    dv_acc[...] = jnp.zeros_like(dv_acc)
+
 
     def dq_args(i):
         t = (lax.rem(y + order(i), 4), c, pw // 4, lax.rem(pw, 4))

time: 85.7 us -> 85.5 us (level)
  no operation moved by 1% of the time
where the time goes in v7:
time: 85.5 us; the launch traced here: 85.4 us
  Pallas kernels  84.8 us (99%)
    pallas_call x1, Pallas kernels, per_device(): pl.pallas_call(kernel, out_shape=(jax.ShapeDtypeStruct((2, 2, BLK, HEAD_D...  82.4 us
    pallas_call x1, Pallas kernels, per_device(): pl.pallas_call(collect, out_shape=(shape, shape, shape), in_specs=[whole]...  2.38 us

profile of v7, /device:TPU:3, one launch (start us, length us, event | category | flops | bytes accessed | tf_op | source)
XLA Modules:
  0.0 85.4 jit_solution(9048873950334230267)
XLA Ops:
  0.6 82.4 %shard_map.67 = (bf16[2,2,768,128]{3,2,1,0:T(8,128)(2,1)}, bf16[768,256]{1,0:T(8,128)(2,1)}, bf16[768,256]{1,0:T(8,128)(2,1)}) custom-call(bf16[768,256]{1,0:T(8,128)(2,1)} %q_in.1, bf16[768,256]{1,0:T(8,128)(2,1)} %k_in.1, bf16[768,256]{1,0:T(8,128)(2,1)} %v_in.1, bf16[768,256]{1,0:T(8,128)(2,1)} %g_in.1), custom_call_target="tpu_custom_call" | custom-call | flops 14495514624 | bytes 1572864 | tf_op jit(solution)/shard_map/pallas_call | solution.py:420
  83.0 2.4 %shard_map.68 = (bf16[768,256]{1,0:T(8,128)(2,1)}, bf16[768,256]{1,0:T(8,128)(2,1)}, bf16[768,256]{1,0:T(8,128)(2,1)}) custom-call(bf16[2,2,768,128]{3,2,1,0:T(8,128)(2,1)} %get-tuple-element.6.dq_raw, bf16[768,256]{1,0:T(8,128)(2,1)} %get-tuple-element.7.dk_raw, bf16[768,256]{1,0:T(8,128)(2,1)} %get-tuple-element.8.dv_raw), custom_call_target="tpu_custom_call" | custom-call | tf_op jit(solution)/shard_map/pallas_call | solution.py:442
